TPU v7x, 32 devices: a whole 2x2x4 slice. The times are simulated.
32 devices in a mesh: groups: 2 (over y), heads: 4 (over z), rows: 4 (over x, core).
Axes of the slice: x: 2, y: 2, z: 4, core: 2. Of those that a mesh axis runs over, the one named last changes fastest.
Arguments:
- queries: bfloat16 [512, 8192], P(('groups', 'heads')), parts along dimension 0, may hold values from -7 to 7
- kv_cache: bfloat16 [2, 4, 16384, 128], P(None, 'groups', ('heads', 'rows')), parts along dimension 1, may hold values from -7 to 7
- start_positions: int32 [4], P('groups'), parts along dimension 0, may hold values from 1024 to 1920, as said below
- residual: bfloat16 [512, 8192], P(('groups', 'heads'), 'rows'), parts along dimension 0, may hold values from -3 to 3
- out_weight: bfloat16 [8192, 8192], P('heads', 'rows'), may hold values from -2 to 2
- norm_gain: float32 [8192], P('rows'), may hold values from 0.1 to 1.9
- gate_weight: bfloat16 [8192, 14336], P('rows', 'heads'), may hold values from -0.0625 to 0.0625
- up_weight: bfloat16 [8192, 14336], P('rows', 'heads'), may hold values from -0.0625 to 0.0625
- down_weight: bfloat16 [14336, 8192], P('heads', 'rows'), may hold values from -0.046875 to 0.046875
Outputs:
- layer_out: bfloat16 [512, 8192], P(('groups', 'heads'), 'rows'), parts along dimension 0
There are 2 independent parts, one for each index of `groups`. A program takes and returns all parts, laid end to end along the dimension named above; an argument that names none is the same for every part. Nothing has to cross between parts.
Inputs may be any that keep to these rules, and one draw needn't show every extreme that they name: Row s * 128 + t of queries is the token at position start_positions[s] + t of sequence s, and the keys and values of the new tokens already stand at those positions of kv_cache; some sequence starts at exactly 1920.
All inputs are finite; a program needn't handle non-finite values.
Results may differ from a plain program's by a relative error of at most 0.017.
Values may be sent and summed in bfloat16 or wider, within the bound.
A program may use at most 128 MiB of HBM per device.

v0:
```python
import math

import jax
import jax.numpy as jnp
from jax import lax
from jax.sharding import PartitionSpec as P

D = 8192
QH = 64
KVH = 8
HD = 128


NEG_FILL = -1e30
EPSILON = 1e-05


def merged(value, axis, join):
    pieces = jax.tree.map(lambda part: lax.all_gather(part, axis), value)
    head = jax.tree.map(lambda part: part[0], pieces)
    tail = jax.tree.map(lambda part: part[1:], pieces)
    so_far, _ = lax.scan(lambda so_far, section: (join(so_far, section), None), head, tail)
    return so_far


def block_scores(query_block, cache_keys, cache_values, start_positions, first_position):
    new_count = query_block.shape[0] // cache_keys.shape[0]
    score_scale = 1.0 / math.sqrt(cache_keys.shape[2])
    positions = first_position + jnp.arange(cache_keys.shape[1], dtype=jnp.int32)
    maxima = []
    totals = []
    blends = []
    for sequence in range(cache_keys.shape[0]):
        rows_here = query_block[sequence * new_count : (sequence + 1) * new_count]
        scores = (
            jnp.einsum(
                "tkd,pd->ktp", rows_here, cache_keys[sequence], preferred_element_type=jnp.float32
            )
            * score_scale
        )
        last_valid = start_positions[sequence] + jnp.arange(new_count, dtype=jnp.int32)
        allowed = (positions[None, :] <= last_valid[:, None])[None]
        scores = jnp.where(allowed, scores, NEG_FILL)
        row_max = jnp.max(scores, axis=-1)
        weights = jnp.where(allowed, jnp.exp(scores - row_max[..., None]), 0.0)
        maxima.append(jnp.transpose(row_max))
        totals.append(jnp.transpose(jnp.sum(weights, axis=-1)))
        blends.append(
            jnp.einsum(
                "ktp,pd->tkd",
                weights.astype(jnp.bfloat16),
                cache_values[sequence],
                preferred_element_type=jnp.float32,
            )
        )
    return (jnp.concatenate(maxima, 0), jnp.concatenate(totals, 0), jnp.concatenate(blends, 0))


def merge_parts(earlier, later):
    joint = jnp.maximum(earlier[0], later[0])
    early_scale = jnp.exp(earlier[0] - joint)
    late_scale = jnp.exp(later[0] - joint)
    return (
        joint,
        earlier[1] * early_scale + later[1] * late_scale,
        earlier[2] * early_scale[..., None] + later[2] * late_scale[..., None],
    )


def local(
    queries,
    kv_cache,
    start_positions,
    residual,
    out_weight,
    norm_gain,
    gate_weight,
    up_weight,
    down_weight,
):
    head_count = lax.axis_size("heads")
    row_count = lax.axis_size("rows")
    head_index = lax.axis_index("heads")
    row_index = lax.axis_index("rows")
    row_block = queries.shape[0]
    total_rows = row_block * head_count
    group_size = QH // KVH
    per_group = head_count * row_count // KVH
    pos_count = kv_cache.shape[2]
    own_shard = head_index * row_count + row_index
    first_position = own_shard % per_group * pos_count
    shard_ids = jnp.arange(head_count, dtype=jnp.int32) * row_count + row_index
    shard_groups = shard_ids // per_group
    grouped = queries.reshape(row_block, KVH, group_size, HD)
    outgoing = jnp.take(grouped, shard_groups, axis=1)
    row_max, weight_sum, blended = block_scores(
        lax.all_to_all(outgoing, "heads", split_axis=1, concat_axis=0, tiled=True)[:, 0],
        kv_cache[0],
        kv_cache[1],
        start_positions,
        first_position,
    )
    got_max, got_sum, got_blend = (
        lax.all_to_all(
            row_max.reshape(head_count, row_block, group_size),
            "heads",
            split_axis=0,
            concat_axis=0,
            tiled=True,
        ),
        lax.all_to_all(
            weight_sum.reshape(head_count, row_block, group_size),
            "heads",
            split_axis=0,
            concat_axis=0,
            tiled=True,
        ),
        lax.all_to_all(
            blended.reshape(head_count, row_block, group_size, HD),
            "heads",
            split_axis=0,
            concat_axis=0,
            tiled=True,
        ),
    )
    member = (shard_groups[:, None] == jnp.arange(KVH, dtype=jnp.int32)[None, :])[:, None, :, None]
    spread_max = jnp.where(member, got_max[:, :, None, :], NEG_FILL)
    canvas_max = jnp.max(spread_max, axis=0)
    factor = jnp.where(member, jnp.exp(got_max[:, :, None, :] - canvas_max[None]), 0.0)
    canvas_sum = jnp.sum(factor * got_sum[:, :, None, :], axis=0)
    canvas_blend = jnp.einsum("srkg,srgd->rkgd", factor, got_blend, precision=lax.Precision.HIGHEST)
    joint_max, joint_sum, joint_blend = merged(
        (canvas_max, canvas_sum, canvas_blend), "rows", merge_parts
    )
    attended = (
        (joint_blend / joint_sum[..., None]).reshape(row_block, head_count, -1).astype(jnp.bfloat16)
    )
    head_rows = lax.all_to_all(attended, "heads", split_axis=1, concat_axis=0, tiled=True).reshape(
        total_rows, -1
    )
    row_start = head_index * row_block
    local_term = jnp.dot(head_rows, out_weight, preferred_element_type=jnp.float32)
    own_rows = lax.dynamic_slice_in_dim(local_term, row_start, row_block, 0) + residual.astype(
        jnp.float32
    )
    local_term = lax.dynamic_update_slice_in_dim(local_term, own_rows, row_start, 0)
    resid_all = lax.psum(local_term, "heads").astype(jnp.bfloat16)
    resid_own = lax.dynamic_slice_in_dim(resid_all, row_start, row_block, 0)
    resid_wide = resid_all.astype(jnp.float32)
    square = jnp.sum(resid_wide * resid_wide, axis=1)
    scaled = (resid_wide * norm_gain).astype(jnp.bfloat16)
    gate_part = jnp.dot(scaled, gate_weight, preferred_element_type=jnp.float32)
    up_part = jnp.dot(scaled, up_weight, preferred_element_type=jnp.float32)
    gate_sum, up_sum, square_sum = lax.psum((gate_part, up_part, square), "rows")
    inverse = lax.rsqrt(square_sum / D + EPSILON)[:, None]
    hidden = (jax.nn.silu(gate_sum * inverse) * (up_sum * inverse)).astype(jnp.bfloat16)
    down_sum = lax.psum_scatter(
        jnp.dot(hidden, down_weight, preferred_element_type=jnp.float32),
        "heads",
        scatter_dimension=0,
        tiled=True,
    )
    return (resid_own.astype(jnp.float32) + down_sum).astype(jnp.bfloat16)


def solution(mesh):
    return jax.shard_map(
        local,
        mesh=mesh,
        in_specs=(
            P(("groups", "heads"), None),
            P(None, "groups", ("heads", "rows"), None),
            P("groups"),
            P(("groups", "heads"), "rows"),
            P("heads", "rows"),
            P("rows"),
            P("rows", "heads"),
            P("rows", "heads"),
            P("heads", "rows"),
        ),
        out_specs=P(("groups", "heads"), "rows"),
        check_vma=False,
    )
```

profile of v0, /device:TPU:17, one launch (start us, length us, event | category | flops | bytes accessed | tf_op | source)
XLA Modules:
  0.0 495.8 jit_solution(7816099900571446197)
XLA Ops:
  9.8 4.6 all-to-all-start
  16.7 8.7 %all-to-all-done = bf16[64,4,8,128]{3,2,0,1:T(8,128)(2,1)S(1)} async-done(((bf16[64,4,8,128]{3,2,0,1:T(8,128)(2,1)}), bf16[64,4,8,128]{3,2,0,1:T(8,128)(2,1)S(1)}, u32[]{:S(2)}, u32[]{:S(2)}) %all-to-all-start) | async-done | bytes 524320 | tf_op jit(solution)/shard_map/all_to_all | solution.py:97
  32.2 6.2 %all-to-all-start.1 = ((f32[4,1,512]{2,1,0:T(1,128)}), f32[4,1,512]{2,1,0:T(1,128)S(1)}, u32[]{:S(2)}, u32[]{:S(2)}) async-start(f32[4,1,512]{2,1,0:T(1,128)} %reshape.225), calls=%async_computation.1 | async-start | bytes 16384 | tf_op jit(solution)/shard_map/all_to_all | solution.py:104
  40.8 5.5 %all-to-all-start.3 = ((f32[4,64,8,128]{3,2,1,0:T(8,128)}), f32[4,64,8,128]{3,2,1,0:T(8,128)S(1)}, u32[]{:S(2)}, u32[]{:S(2)}) async-start(f32[4,64,8,128]{3,2,1,0:T(8,128)} %copy.75), calls=%async_computation.3 | async-start | bytes 2097152 | tf_op jit(solution)/shard_map/all_to_all | solution.py:118
  48.7 19.9 %all-to-all-done.3 = f32[4,64,8,128]{3,2,1,0:T(8,128)S(1)} async-done(((f32[4,64,8,128]{3,2,1,0:T(8,128)}), f32[4,64,8,128]{3,2,1,0:T(8,128)S(1)}, u32[]{:S(2)}, u32[]{:S(2)}) %all-to-all-start.3) | async-done | bytes 1048608 | tf_op jit(solution)/shard_map/all_to_all | solution.py:118
  68.6 5.3 %convolution_bitcast_fusion = f32[64,8,8,128]{3,1,2,0:T(8,128)S(1)} fusion(f32[4,64,8,128]{3,2,1,0:T(8,128)S(1)} %all-to-all-done.3, f32[64,8,8]{1,2,0:T(8,128)S(1)} %select_reduce_fusion, f32[4,64,8]{0,2,1:T(8,128)S(1)} %copy.70, pred[4,8]{1,0:T(4,128)(4,1)S(1)} %iota_compare_fusion), kind=kOutput, calls=%fused_computation.38 | convolution fusion | flops 25198592 | bytes 3170336 | tf_op jit(solution)/shard_map/srkg,srgd->rkgd/dot_general | solution.py:131
  75.7 4.9 fusion.8
  81.4 6.2 %all-to-all-start.2 = ((f32[4,1,512]{2,1,0:T(1,128)}), f32[4,1,512]{2,1,0:T(1,128)S(1)}, u32[]{:S(2)}, u32[]{:S(2)}) async-start(f32[4,1,512]{2,1,0:T(1,128)} %reshape.227), calls=%async_computation.2 | async-start | bytes 16384 | tf_op jit(solution)/shard_map/all_to_all | solution.py:111
  87.7 17.7 %all-gather = f32[256,8,8]{2,1,0:T(8,128)S(1)} all-gather(f32[64,8,8]{2,1,0:T(8,128)S(1)} %copy.71), channel_id=2, replica_groups=mesh['groups'=2,'heads'=4,'rows'=4] {'rows'}, dimensions={0}, use_global_device_ids=true | all-gather | bytes 81920 | tf_op jit(solution)/shard_map/all_gather | solution.py:19
  107.8 16.4 %all-gather.1 = f32[256,8,8]{2,1,0:T(8,128)S(1)} all-gather(f32[64,8,8]{2,1,0:T(8,128)S(1)} %copy.74), channel_id=3, replica_groups=mesh['groups'=2,'heads'=4,'rows'=4] {'rows'}, dimensions={0}, use_global_device_ids=true | all-gather | bytes 81920 | tf_op jit(solution)/shard_map/all_gather | solution.py:19
  125.1 23.3 %all-gather.5.cloned.1.call-done = f32[256,8,8,128]{3,2,1,0:T(8,128)} async-done(((f32[64,8,8,128]{3,2,1,0:T(8,128)}), f32[256,8,8,128]{3,2,1,0:T(8,128)}) %all-gather.5.cloned.1.call-update) | async-done | bytes 8388624 | tf_op jit(solution)/shard_map/all_gather | solution.py:19
  148.4 6.8 %slice.89 = f32[192,8,8,128]{3,2,1,0:T(8,128)} slice(f32[256,8,8,128]{3,2,1,0:T(8,128)} %all-gather.5.cloned.1.call-done), slice={[64:256], [0:8], [0:8], [0:128]} | slice | bytes 12582912 | tf_op jit(solution)/shard_map/slice | solution.py:21
  155.2 9.2 %while.14 = (s32[]{:T(128)}, f32[64,8,8]{0,2,1:T(8,128)S(1)}, f32[64,8,8]{0,2,1:T(8,128)S(1)}, f32[64,8,8,128]{3,2,1,0:T(8,128)S(1)}, f32[3,64,8,8]{1,3,2,0:T(8,...) while((s32[]{:T(128)}, f32[64,8,8]{0,2,1:T(8,128)S(1)}, ...), condition=%wide.region_7.8_spmd, body=%wide.region_6.7_spmd.sunk | while | flops 1597442 | bytes 6520933 | solution.py:22
  155.5 2.7 fusion.72
  167.1 4.6 all-to-all-start.4
  171.7 22.3 %all-to-all-done.4 = bf16[64,4,2048]{2,0,1:T(8,128)(2,1)S(1)} async-done(((bf16[64,4,2048]{2,0,1:T(8,128)(2,1)}), bf16[64,4,2048]{2,0,1:T(8,128)(2,1)S(1)}, u32[]{:S(2)}, u32[]{:S(2)}) %all-to-all-start.4) | async-done | bytes 1048608 | tf_op jit(solution)/shard_map/all_to_all | solution.py:138
  194.0 5.7 %fusion.61 = f32[256,2048]{1,0:T(8,128)S(1)} fusion(bf16[256,2048]{1,0:T(8,128)(2,1)S(1)} %bitcast.134, bf16[2048,2048]{1,0:T(8,128)(2,1)} %param.15), kind=kOutput, calls=%fused_computation.99 | convolution fusion | flops 2147483648 | bytes 11534336 | tf_op jit(solution)/shard_map/dot_general | solution.py:142
  199.9 73.9 %all-reduce.5 = bf16[256,2048]{1,0:T(8,128)(2,1)S(1)} all-reduce(f32[256,2048]{1,0:T(8,128)S(1)} %add_dynamic-update-slice_fusion), channel_id=1, replica_groups=mesh['groups'=2,'heads'=4,'rows'=4] {'heads'}, use_global_device_ids=true, to_apply=%region_8.9 | all-reduce | flops 524288 | bytes 3145728 | tf_op jit(solution)/shard_map/psum | solution.py:147
  273.8 9.2 %fusion.33 = f32[256,3584]{1,0:T(8,128)} fusion(bf16[2048,3584]{1,0:T(8,128)(2,1)} %param.17, bf16[256,2048]{1,0:T(8,128)(2,1)S(1)} %all-reduce.5, f32[2048]{0:T(1024)S(1)} %copy-done.5), kind=kOutput, calls=%fused_computation.47 | convolution fusion | flops 3759669248 | bytes 19406848 | tf_op jit(solution)/shard_map/dot_general | solution.py:152
  282.9 9.1 %fusion.31 = f32[256,3584]{1,0:T(8,128)} fusion(bf16[2048,3584]{1,0:T(8,128)(2,1)} %param.18, bf16[256,2048]{1,0:T(8,128)(2,1)S(1)} %all-reduce.5, f32[2048]{0:T(1024)S(1)} %copy-done.5), kind=kOutput, calls=%fused_computation.46 | convolution fusion | flops 3759669248 | bytes 19406848 | tf_op jit(solution)/shard_map/dot_general | solution.py:153
  292.4 8.6 %psum.30 = f32[256]{0:T(256)S(1)} all-reduce(f32[256]{0:T(256)S(1)} %fusion.12), channel_id=1, replica_groups=mesh['groups'=2,'heads'=4,'rows'=4] {'rows'}, use_global_device_ids=true, to_apply=%region_11.12 | all-reduce | flops 256 | bytes 2048 | tf_op jit(solution)/shard_map/psum | solution.py:154
  301.1 129.5 %all-reduce.4.cloned.1.call-done = (f32[256,3584]{1,0:T(8,128)}, f32[256,3584]{1,0:T(8,128)}) async-done(((f32[256,3584]{1,0:T(8,128)}, f32[256,3584]{1,0:T(8,128)}), (f32[256,3584]{1,0:T(8,128)}, f32[256,3584]{1,0:T(8,128)})) %all-reduce.4.cloned.1.call-update) | async-done | bytes 7340048 | tf_op jit(solution)/shard_map/psum | solution.py:154
  430.6 12.9 %fusion.21 = f32[256,2048]{1,0:T(8,128)} fusion(bf16[3584,2048]{1,0:T(8,128)(2,1)} %param.19, f32[256,3584]{1,0:T(8,128)} %get-tuple-element.94, f32[256,3584]{1,0:T(8,128)} %get-tuple-element.95, f32[256]{0:T(256)S(1)} %add_rsqrt_fusion), kind=kOutput, calls=%fused_computation.35 | convolution fusion | flops 3765436416 | bytes 24118272 | tf_op jit(solution)/shard_map/dot_general | solution.py:158
  443.5 43.9 %reduce-scatter.2.cloned.1.call-done = f32[64,2048]{1,0:T(8,128)} async-done(((f32[256,2048]{1,0:T(8,128)}), f32[64,2048]{1,0:T(8,128)}) %reduce-scatter.2.cloned.1.call-update) | async-done | bytes 524304 | tf_op jit(solution)/shard_map/reduce_scatter | solution.py:157
  (91 shorter events, 34.2 us)
Async XLA Ops:
  6.5 7.9 %copy-start.4 = (s32[2]{0:T(128)S(1)}, s32[2]{0:T(128)}, u32[]{:S(2)}) copy-start(s32[2]{0:T(128)} %param.13) | copy-start | bytes 28
  6.5 19.1 %copy-start.2 = (bf16[2,2,1024,128]{3,2,1,0:T(8,128)(2,1)S(1)}, bf16[2,2,1024,128]{3,2,1,0:T(8,128)(2,1)}, u32[]{:S(2)}) copy-start(bf16[2,2,1024,128]{3,2,1,0:T(8,128)(2,1)} %param.12) | copy-start | bytes 3145732
  9.8 15.7 %all-to-all-start = ((bf16[64,4,8,128]{3,2,0,1:T(8,128)(2,1)}), bf16[64,4,8,128]{3,2,0,1:T(8,128)(2,1)S(1)}, u32[]{:S(2)}, u32[]{:S(2)}) async-start(bf16[64,4,8,128]{3,2,0,1:T(8,128)(2,1)} %select_bitcast_fusion), calls=%async_computation | async-start | bytes 1048576 | tf_op jit(solution)/shard_map/all_to_all | solution.py:97
  26.6 2.0 copy-start
  29.5 2.0 copy-start.1
  32.2 8.6 %all-to-all-start.1 = ((f32[4,1,512]{2,1,0:T(1,128)}), f32[4,1,512]{2,1,0:T(1,128)S(1)}, u32[]{:S(2)}, u32[]{:S(2)}) async-start(f32[4,1,512]{2,1,0:T(1,128)} %reshape.225), calls=%async_computation.1 | async-start | bytes 16384 | tf_op jit(solution)/shard_map/all_to_all | solution.py:104
  40.8 27.8 %all-to-all-start.3 = ((f32[4,64,8,128]{3,2,1,0:T(8,128)}), f32[4,64,8,128]{3,2,1,0:T(8,128)S(1)}, u32[]{:S(2)}, u32[]{:S(2)}) async-start(f32[4,64,8,128]{3,2,1,0:T(8,128)} %copy.75), calls=%async_computation.3 | async-start | bytes 2097152 | tf_op jit(solution)/shard_map/all_to_all | solution.py:118
  46.4 102.0 %all-gather.5.cloned.1.call-start = ((), (), s32[]{:S(2)}) async-start(), calls=%async_computation.7 | async-start | bytes 10485760 | tf_op jit(solution)/shard_map/all_gather | solution.py:19
  81.4 24.1 %all-to-all-start.2 = ((f32[4,1,512]{2,1,0:T(1,128)}), f32[4,1,512]{2,1,0:T(1,128)S(1)}, u32[]{:S(2)}, u32[]{:S(2)}) async-start(f32[4,1,512]{2,1,0:T(1,128)} %reshape.227), calls=%async_computation.2 | async-start | bytes 16384 | tf_op jit(solution)/shard_map/all_to_all | solution.py:111
  148.4 6.8 %slice-start = ((f32[256,8,8,128]{3,2,1,0:T(8,128)}), f32[64,8,8,128]{3,2,1,0:T(8,128)S(1)}, s32[]{:S(2)}) async-start(f32[256,8,8,128]{3,2,1,0:T(8,128)} %all-gather.5.cloned.1.call-done), calls=%async_computation.9 | async-start | bytes 4194304 | tf_op jit(solution)/shard_map/slice | solution.py:20
  167.1 26.9 %all-to-all-start.4 = ((bf16[64,4,2048]{2,0,1:T(8,128)(2,1)}), bf16[64,4,2048]{2,0,1:T(8,128)(2,1)S(1)}, u32[]{:S(2)}, u32[]{:S(2)}) async-start(bf16[64,4,2048]{2,0,1:T(8,128)(2,1)} %copy.85), calls=%async_computation.4 | async-start | bytes 2097152 | tf_op jit(solution)/shard_map/all_to_all | solution.py:138
  171.7 258.9 %all-reduce.4.cloned.1.call-start = ((), (), s32[]{:S(2)}) async-start(), calls=%async_computation.8 | async-start | bytes 14680064 | tf_op jit(solution)/shard_map/psum | solution.py:154
  194.0 5.8 %copy-start.3 = (bf16[64,2048]{1,0:T(8,128)(2,1)S(1)}, bf16[64,2048]{1,0:T(8,128)(2,1)}, u32[]{:S(2)}) copy-start(bf16[64,2048]{1,0:T(8,128)(2,1)} %param.14) | copy-start | bytes 786436
  199.8 74.0 %copy-start.5 = (f32[2048]{0:T(1024)S(1)}, f32[2048]{0:T(1024)}, u32[]{:S(2)}) copy-start(f32[2048]{0:T(1024)} %param.16) | copy-start | bytes 24580
  292.1 195.3 %reduce-scatter.2.cloned.1.call-start = ((), (), s32[]{:S(2)}) async-start(), calls=%async_computation.6 | async-start | bytes 2621440 | tf_op jit(solution)/shard_map/reduce_scatter | solution.py:157
Sparse Core Ops, SparseCore 0:
  75.8 72.5 all-gather.4
  292.2 138.2 all-reduce.3
  443.7 43.7 reduce-scatter.1
where the time goes:
time: 499 us; the launch traced here: 496 us
  waiting for transfers between devices  248 us (50%)
  blocking collectives  117 us (23%)
  matrix products  46.7 us (9%)
  starting transfers between devices  27.2 us (5%)
  other arithmetic  22 us (4%)
  local copies, waits for them, and re-layouts  21.3 us (4%)
  between operations  13.4 us (3%)
    psum x1, waiting for transfers between devices, local(): lax.psum((gate_part, up_part, square), 'rows')  130 us
    psum x1, blocking collectives, local(): resid_all = lax.psum(local_term, 'heads').astype(jnp.bfloat16)  73.9 us
    reduce_scatter x1, waiting for transfers between devices, local(): lax.psum_scatter(jnp.dot(hidden, down_weight, preferred_element_type=jnp....  43.9 us
    all_gather x2, blocking collectives, merged(): pieces = jax.tree.map(lambda part: lax.all_gather(part, axis), value)  34 us
    all_gather x1, waiting for transfers between devices, merged(): pieces = jax.tree.map(lambda part: lax.all_gather(part, axis), value)  23.3 us
    all_to_all x1, waiting for transfers between devices, local(): lax.all_to_all(attended, 'heads', split_axis=1, concat_axis=0, tiled=True)  22.3 us
    all_to_all x1, waiting for transfers between devices, local(): lax.all_to_all(blended.reshape(head_count, row_block, group_size, HD), 'h...  19.9 us
    dot_general x1, matrix products, local(): jnp.dot(hidden, down_weight, preferred_element_type=jnp.float32)  12.9 us
  transfers between devices with their start and end apart: 8, of which 7 were waited for; matrix products, arithmetic and copies ran while one was open for 3% of the time, Pallas kernels for 0%

commit v1 on v0

--- a/solution.py
+++ b/solution.py
@@ -2,6 +2,8 @@
 
 import jax
 import jax.numpy as jnp
+import jax.experimental.pallas as pl
+import jax.experimental.pallas.tpu as pltpu
 from jax import lax
 from jax.sharding import PartitionSpec as P
 
@@ -13,6 +15,7 @@
 
 NEG_FILL = -1e30
 EPSILON = 1e-05
+MESH = pl.DeviceIdType.MESH
 
 
 def merged(value, axis, join):
@@ -92,7 +95,15 @@
     shard_ids = jnp.arange(head_count, dtype=jnp.int32) * row_count + row_index
     shard_groups = shard_ids // per_group
     grouped = queries.reshape(row_block, KVH, group_size, HD)
-    outgoing = jnp.take(grouped, shard_groups, axis=1)
+    outgoing = jnp.stack(
+        [
+            lax.dynamic_index_in_dim(
+                grouped, (i * row_count + row_index) // per_group, 1, keepdims=False
+            )
+            for i in range(head_count)
+        ],
+        axis=1,
+    )
     row_max, weight_sum, blended = block_scores(
         lax.all_to_all(outgoing, "heads", split_axis=1, concat_axis=0, tiled=True)[:, 0],
         kv_cache[0],
@@ -163,9 +174,436 @@
     return (resid_own.astype(jnp.float32) + down_sum).astype(jnp.bfloat16)
 
 
+def fused_kernel(
+    q_hbm, kv_hbm, start_ref, res_hbm, wo_hbm, gain_ref, wg_hbm, wu_hbm, wd_hbm, out_ref,
+    wo, wg, wu, wd2, qbuf, kvbuf, attn, zsend, zrecv, resid, res, scl, gsend, grecv,
+    xrecv, hid, sqs, sqr, sqx,
+    lsem, qss, qrs, kss, krs, asx, arx, asc, arc, asf, arf, zss, zrs, rss, rrs, gss, grs,
+    xss, xrs, sss, srs, hsx, hrx, hsc, hrc, hsf, hrf, dss, drs,
+):
+    h = lax.axis_index("heads")
+    r = lax.axis_index("rows")
+    x = r // 2
+    c = r % 2
+    core_peer = x * 2 + (1 - c)
+    chip_peer = (1 - x) * 2 + c
+    block = zrecv.shape[2]
+    span = 4 * block
+    pair = 2 * block
+    width = qbuf.shape[2]
+    depth = wo.shape[1]
+    quarter = hid.shape[2] // 4
+    first = wo.shape[0]
+
+    def remote(src, dst, ss, rs, hh, rr):
+        return pltpu.make_async_remote_copy(
+            src_ref=src, dst_ref=dst, send_sem=ss, recv_sem=rs,
+            device_id={"heads": hh, "rows": rr}, device_id_type=MESH,
+        )
+
+    def lanes(start, size):
+        return pl.ds(pl.multiple_of(start, 128), size)
+
+    def subl(start, size):
+        return pl.ds(pl.multiple_of(start, 32), size)
+
+    def ring(d):
+        return lax.rem(h + d, 4)
+
+    kv_own = pltpu.make_async_copy(kv_hbm.at[:, c], kvbuf.at[:, c], lsem.at[0])
+    kv_own.start()
+    q_own = pltpu.make_async_copy(
+        q_hbm.at[:, :, lanes((2 * h + x) * width, width)],
+        qbuf.at[:, subl(lax.rem(h, 2) * block, block), :],
+        lsem.at[1],
+    )
+    sender = c == h // 2
+
+    @pl.when(sender)
+    def _():
+        q_own.start()
+
+    barrier = pltpu.get_barrier_semaphore()
+    for d in (1, 2, 3):
+        pl.semaphore_signal(
+            barrier, inc=1, device_id={"heads": ring(d), "rows": r}, device_id_type=MESH
+        )
+        pl.semaphore_signal(
+            barrier, inc=1, device_id={"heads": h, "rows": lax.rem(r + d, 4)}, device_id_type=MESH
+        )
+    pl.semaphore_wait(barrier, 6)
+
+    def q_copy(d):
+        hh = ring(d)
+        return remote(
+            q_hbm.at[:, :, lanes((2 * hh + x) * width, width)],
+            qbuf.at[:, subl(lax.rem(h, 2) * block, block), :],
+            qss.at[d - 1], qrs.at[lax.rem(h, 2)], hh, r,
+        )
+
+    @pl.when(sender)
+    def _():
+        for d in (2, 1, 3):
+            q_copy(d).start()
+
+    kv_copy = remote(kv_hbm.at[:, 1 - c], kvbuf.at[:, c], kss.at[0], krs.at[0], h, core_peer)
+    kv_copy.start()
+
+    res_load = pltpu.make_async_copy(res_hbm, res, lsem.at[2])
+    wo_load = pltpu.make_async_copy(wo_hbm, wo, lsem.at[3])
+    wg_load = pltpu.make_async_copy(wg_hbm, wg, lsem.at[4])
+    wu_load = pltpu.make_async_copy(wu_hbm, wu, lsem.at[5])
+    wd2_load = pltpu.make_async_copy(
+        wd_hbm.at[pl.ds(first, wd2.shape[0]), :], wd2, lsem.at[6]
+    )
+    wd1_load = pltpu.make_async_copy(wd_hbm.at[pl.ds(0, first), :], wo, lsem.at[7])
+    for load in (res_load, wo_load, wg_load, wu_load, wd2_load):
+        load.start()
+
+    kv_own.wait()
+    remote(
+        kv_hbm.at[:, 1 - c], kvbuf.at[:, 1 - c], kss.at[0], krs.at[0], h, core_peer
+    ).wait_recv()
+    for j in (0, 1):
+        here = sender & (lax.rem(h, 2) == j)
+
+        @pl.when(here)
+        def _():
+            q_own.wait()
+
+        @pl.when(jnp.logical_not(here))
+        def _():
+            remote(
+                q_hbm.at[:, :, pl.ds(0, width)], qbuf.at[:, pl.ds(j * block, block), :],
+                qss.at[0], qrs.at[j], ring(1), r,
+            ).wait_recv()
+
+    scale = 1.0 / math.sqrt(HD)
+    start = start_ref[c]
+    positions = kvbuf.shape[1] * kvbuf.shape[2]
+
+    def head_body(k, half):
+        row = lax.broadcasted_iota(jnp.int32, (pair, 1), 0)
+        token = (row // block) * pair + half * block + row % block
+        col = lax.broadcasted_iota(jnp.int32, (pair, positions), 1)
+        allowed = col <= start + token
+        s = lax.dot_general(
+            qbuf[half, :, lanes(k * HD, HD)], kvbuf[0].reshape(positions, HD),
+            (((1,), (1,)), ((), ())), preferred_element_type=jnp.float32,
+        ) * scale
+        s = jnp.where(allowed, s, NEG_FILL)
+        p = jnp.exp(s - jnp.max(s, axis=1, keepdims=True))
+        total = jnp.sum(p, axis=1, keepdims=True)
+        o = jnp.dot(
+            p.astype(jnp.bfloat16), kvbuf[1].reshape(positions, HD),
+            preferred_element_type=jnp.float32,
+        )
+        attn[half, subl(c * pair, pair), lanes(x * width + k * HD, HD)] = (o / total).astype(
+            jnp.bfloat16
+        )
+
+    piece = width // 4
+
+    def attn_block(cc, xx, ch):
+        return attn.at[:, subl(cc * pair, pair), lanes(xx * width + ch * piece, piece)]
+
+    def attn_body(ch, carry):
+        for k in range(piece // HD):
+            for half in (0, 1):
+                head_body(ch * (piece // HD) + k, half)
+        mine = attn_block(c, x, ch)
+        remote(mine, mine, asx.at[ch], arx.at[ch], h, chip_peer).start()
+        remote(mine, mine, asc.at[ch], arc.at[ch], h, core_peer).start()
+        return carry
+
+    lax.fori_loop(0, 4, attn_body, 0)
+
+    def forward_body(ch, carry):
+        far = attn_block(c, 1 - x, ch)
+        remote(far, far, asx.at[ch], arx.at[ch], h, chip_peer).wait_recv()
+        remote(far, far, asf.at[ch], arf.at[ch], h, core_peer).start()
+        return carry
+
+    lax.fori_loop(0, 4, forward_body, 0)
+
+    def gathered_body(ch, carry):
+        near = attn_block(1 - c, x, ch)
+        far = attn_block(1 - c, 1 - x, ch)
+        remote(near, near, asc.at[ch], arc.at[ch], h, core_peer).wait_recv()
+        remote(far, far, asf.at[ch], arf.at[ch], h, core_peer).wait_recv()
+        mine = attn_block(c, x, ch)
+        remote(mine, mine, asx.at[ch], arx.at[ch], h, chip_peer).wait_send()
+        remote(mine, mine, asc.at[ch], arc.at[ch], h, core_peer).wait_send()
+        remote(mine, mine, asf.at[ch], arf.at[ch], h, core_peer).wait_send()
+        return carry
+
+    lax.fori_loop(0, 4, gathered_body, 0)
+    wo_load.wait()
+    res_load.wait()
+    cols = 512
+
+    def z_copy(half, d, target, ss, rs):
+        hh = ring(d)
+        return remote(
+            zsend.at[half, subl(hh * block, block), :], target.at[half, d - 1],
+            ss.at[half, d - 1], rs.at[half, d - 1], hh, r,
+        )
+
+    def project_body(half, carry):
+        def chunk(n, inner):
+            part = jnp.dot(
+                attn[half], wo[:, lanes(n * cols, cols)], preferred_element_type=jnp.float32
+            )
+            zsend[half, :, lanes(n * cols, cols)] = part.astype(jnp.bfloat16)
+            return inner
+
+        lax.fori_loop(0, depth // cols, chunk, 0)
+        for d in (2, 1, 3):
+            z_copy(half, d, zrecv, zss, zrs).start()
+        return carry
+
+    lax.fori_loop(0, 2, project_body, 0)
+    wd1_load.start()
+
+    def r_copy(half, d, source):
+        mine = resid.at[half, subl(source * block, block), :]
+        return remote(mine, mine, rss.at[half, d - 1], rrs.at[half, d - 1], ring(d), r)
+
+    def resid_body(half, carry):
+        for d in (1, 2, 3):
+            z_copy(half, d, zrecv, zss, zrs).wait_recv()
+        total = zsend[half, subl(h * block, block), :].astype(jnp.float32)
+        for d in (1, 2, 3):
+            total = total + zrecv[half, d - 1].astype(jnp.float32)
+        total = total + res[half].astype(jnp.float32)
+        resid[half, subl(h * block, block), :] = total.astype(jnp.bfloat16)
+        for d in (2, 1, 3):
+            r_copy(half, d, h).start()
+        return carry
+
+    lax.fori_loop(0, 2, resid_body, 0)
+    wg_load.wait()
+    wu_load.wait()
+
+    def both(qi):
+        at = lanes(qi * quarter, quarter)
+        return (
+            jnp.dot(scl[...], wg[:, at], preferred_element_type=jnp.float32),
+            jnp.dot(scl[...], wu[:, at], preferred_element_type=jnp.float32),
+        )
+
+    def g_copy(half, xx):
+        return remote(
+            gsend.at[xx], grecv.at[half, xx], gss.at[half, xx], grs.at[half, xx], h, core_peer
+        )
+
+    def sq_copy(half):
+        return remote(sqs.at[half], sqr.at[half], sss.at[half, 0], srs.at[half, 0], h, core_peer)
+
+    def sq_copy2(half):
+        return remote(sqr.at[half], sqx.at[half], sss.at[half, 1], srs.at[half, 1], h, chip_peer)
+
+    def x_copy(half):
+        return remote(grecv.at[half, 1 - x], xrecv.at[half], xss.at[half], xrs.at[half], h, chip_peer)
+
+    def gate_body(half, carry):
+        for d in (1, 2, 3):
+            r_copy(half, d, lax.rem(h + 4 - d, 4)).wait_recv()
+        wide = resid[half].astype(jnp.float32)
+        sqs[half] = jnp.broadcast_to(jnp.sum(wide * wide, axis=1, keepdims=True), (span, 128))
+        sq_copy(half).start()
+        scl[...] = (wide * gain_ref[...]).astype(jnp.bfloat16)
+
+        @pl.when(half == 1)
+        def _():
+            for xx in (0, 1):
+                g_copy(0, xx).wait_send()
+
+        def partner(i, inner):
+            xx = lax.rem(1 - x + i, 2)
+            g, u = both(2 * xx + 1 - c)
+            gsend[xx, :, 0:quarter] = g.astype(jnp.bfloat16)
+            gsend[xx, :, quarter:] = u.astype(jnp.bfloat16)
+            g_copy(half, xx).start()
+            return inner
+
+        lax.fori_loop(0, 2, partner, 0)
+        g, u = both(2 * (1 - x) + c)
+        g_copy(half, 1 - x).wait_recv()
+        grecv[half, 1 - x, :, 0:quarter] = (
+            g + grecv[half, 1 - x, :, 0:quarter].astype(jnp.float32)
+        ).astype(jnp.bfloat16)
+        grecv[half, 1 - x, :, quarter:] = (
+            u + grecv[half, 1 - x, :, quarter:].astype(jnp.float32)
+        ).astype(jnp.bfloat16)
+        x_copy(half).start()
+        sq_copy(half).wait_recv()
+        sqr[half] = sqs[half] + sqr[half]
+        sq_copy2(half).start()
+        g, u = both(2 * x + c)
+        g_copy(half, x).wait_recv()
+        grecv[half, x, :, 0:quarter] = (
+            g + grecv[half, x, :, 0:quarter].astype(jnp.float32)
+        ).astype(jnp.bfloat16)
+        grecv[half, x, :, quarter:] = (
+            u + grecv[half, x, :, quarter:].astype(jnp.float32)
+        ).astype(jnp.bfloat16)
+        return carry
+
+    lax.fori_loop(0, 2, gate_body, 0)
+
+    def h_copy(half, owner, ss, rs, rr):
+        mine = hid.at[half, :, lanes(owner * quarter, quarter)]
+        return remote(mine, mine, ss.at[half], rs.at[half], h, rr)
+
+    def hidden_body(half, carry):
+        x_copy(half).wait_recv()
+        sq_copy2(half).wait_recv()
+        square = (sqr[half] + sqx[half])[:, 0:1]
+        inverse = lax.rsqrt(square / D + EPSILON)
+        summed = grecv[half, x].astype(jnp.float32) + xrecv[half].astype(jnp.float32)
+        gate = summed[:, 0:quarter] * inverse
+        up = summed[:, quarter:] * inverse
+        hid[half, :, lanes(r * quarter, quarter)] = (gate / (1.0 + jnp.exp(-gate)) * up).astype(
+            jnp.bfloat16
+        )
+        h_copy(half, r, hsx, hrx, chip_peer).start()
+        h_copy(half, r, hsc, hrc, core_peer).start()
+        return carry
+
+    lax.fori_loop(0, 2, hidden_body, 0)
+    wd1_load.wait()
+    wd2_load.wait()
+
+    def down_body(half, carry):
+        h_copy(half, chip_peer, hsx, hrx, chip_peer).wait_recv()
+        h_copy(half, chip_peer, hsf, hrf, core_peer).start()
+        for d in (1, 2, 3):
+            z_copy(half, d, zrecv, zss, zrs).wait_send()
+        h_copy(half, core_peer, hsc, hrc, core_peer).wait_recv()
+        h_copy(half, 2 * (1 - x) + 1 - c, hsf, hrf, core_peer).wait_recv()
+
+        def chunk(n, inner):
+            at = lanes(n * cols, cols)
+            part = jnp.dot(
+                hid[half, :, 0:first], wo[:, at], preferred_element_type=jnp.float32
+            ) + jnp.dot(hid[half, :, first:], wd2[:, at], preferred_element_type=jnp.float32)
+            zsend[half, :, at] = part.astype(jnp.bfloat16)
+            return inner
+
+        lax.fori_loop(0, depth // cols, chunk, 0)
+        for d in (2, 1, 3):
+            z_copy(half, d, zrecv, dss, drs).start()
+        return carry
+
+    lax.fori_loop(0, 2, down_body, 0)
+
+    def final_body(half, carry):
+        for d in (1, 2, 3):
+            z_copy(half, d, zrecv, dss, drs).wait_recv()
+        total = zsend[half, subl(h * block, block), :].astype(jnp.float32)
+        for d in (1, 2, 3):
+            total = total + zrecv[half, d - 1].astype(jnp.float32)
+        total = total + resid[half, subl(h * block, block), :].astype(jnp.float32)
+        out_ref[half] = total.astype(jnp.bfloat16)
+        return carry
+
+    lax.fori_loop(0, 2, final_body, 0)
+
+    @pl.when(sender)
+    def _():
+        for d in (1, 2, 3):
+            q_copy(d).wait_send()
+
+    kv_copy.wait_send()
+
+    def drain(half, carry):
+        for d in (1, 2, 3):
+            r_copy(half, d, h).wait_send()
+            z_copy(half, d, zrecv, dss, drs).wait_send()
+        sq_copy(half).wait_send()
+        sq_copy2(half).wait_send()
+        x_copy(half).wait_send()
+        h_copy(half, r, hsx, hrx, chip_peer).wait_send()
+        h_copy(half, r, hsc, hrc, core_peer).wait_send()
+        h_copy(half, chip_peer, hsf, hrf, core_peer).wait_send()
+        return carry
+
+    lax.fori_loop(0, 2, drain, 0)
+    for xx in (0, 1):
+        g_copy(1, xx).wait_send()
+
+
+def fused(
+    queries, kv_cache, start_positions, residual, out_weight, norm_gain, gate_weight, up_weight,
+    down_weight,
+):
+    rows, wide = queries.shape
+    block = rows // 2
+    span = 4 * block
+    width = wide // KVH
+    depth = residual.shape[1]
+    units = gate_weight.shape[1]
+    quarter = units // 4
+    first = out_weight.shape[0]
+    half_rest = units - first
+    bf, f32 = jnp.bfloat16, jnp.float32
+    vmem, dma = pltpu.VMEM, pltpu.SemaphoreType.DMA
+    anyspace = pl.BlockSpec(memory_space=pl.ANY)
+    vspec = pl.BlockSpec(memory_space=pltpu.VMEM)
+    out = pl.pallas_call(
+        fused_kernel,
+        out_shape=jax.ShapeDtypeStruct((2, block, depth), bf),
+        in_specs=[
+            anyspace, anyspace, pl.BlockSpec(memory_space=pltpu.SMEM), anyspace, anyspace, vspec,
+            anyspace, anyspace, anyspace,
+        ],
+        out_specs=vspec,
+        scratch_shapes=[
+            vmem((first, depth), bf),
+            vmem((depth, units), bf),
+            vmem((depth, units), bf),
+            vmem((half_rest, depth), bf),
+            vmem((2, 2 * block, width), bf),
+            vmem(kv_cache.shape, bf),
+            vmem((2, span, 2 * width), bf),
+            vmem((2, span, depth), bf),
+            vmem((2, 3, block, depth), bf),
+            vmem((2, span, depth), bf),
+            vmem((2, block, depth), bf),
+            vmem((span, depth), bf),
+            vmem((2, span, 2 * quarter), bf),
+            vmem((2, 2, span, 2 * quarter), bf),
+            vmem((2, span, 2 * quarter), bf),
+            vmem((2, span, units), bf),
+            vmem((2, span, 128), f32),
+            vmem((2, span, 128), f32),
+            vmem((2, span, 128), f32),
+            dma((8,)), dma((3,)), dma((2,)), dma((1,)), dma((1,)),
+            dma((4,)), dma((4,)), dma((4,)), dma((4,)), dma((4,)), dma((4,)),
+            dma((2, 3)), dma((2, 3)), dma((2, 3)), dma((2, 3)),
+            dma((2, 2)), dma((2, 2)), dma((2,)), dma((2,)), dma((2, 2)), dma((2, 2)),
+            dma((2,)), dma((2,)), dma((2,)), dma((2,)), dma((2,)), dma((2,)),
+            dma((2, 3)), dma((2, 3)),
+        ],
+        compiler_params=pltpu.CompilerParams(
+            collective_id=0, has_side_effects=True, vmem_limit_bytes=63 * 1024 * 1024
+        ),
+    )(
+        queries.reshape(2, block, wide), kv_cache, start_positions,
+        residual.reshape(2, block, depth), out_weight, norm_gain.reshape(1, depth), gate_weight,
+        up_weight, down_weight,
+    )
+    return out.reshape(rows, depth)
+
+
+def one_kernel_fits(mesh):
+    return mesh.shape["heads"] == 4 and mesh.shape["rows"] == 4
+
+
 def solution(mesh):
     return jax.shard_map(
-        local,
+        fused if one_kernel_fits(mesh) else local,
         mesh=mesh,
         in_specs=(
             P(("groups", "heads"), None),

time: 499 us -> 131 us (0.26)
  waiting for transfers between devices: 248 us -> 0 us
  Pallas kernels: 0 us -> 130 us
  blocking collectives: 117 us -> 0 us
  matrix products: 46.7 us -> 0 us
  starting transfers between devices: 27.2 us -> 0 us
  other arithmetic: 22 us -> 0 us
  local copies, waits for them, and re-layouts: 21.3 us -> 1.67 us
  between operations: 13.4 us -> 0.01 us
    pallas_call x0 -> x1, Pallas kernels: none -> 130 us  [fused(): pl.pallas_call(fused_kernel, out_shape=jax.ShapeDtypeStruct((2, block, de...]
    psum x1 -> x0, waiting for transfers between devices: 130 us -> none  [local(): lax.psum((gate_part, up_part, square), 'rows')]
    psum x2 -> x0, blocking collectives: 82.5 us -> none  [the longest x1 73.9 us: local(): resid_all = lax.psum(local_term, 'heads').astype(jnp.bfloat16)]
    all_to_all x5 -> x0, waiting for transfers between devices: 51.7 us -> none  [the longest x1 22.3 us: local(): lax.all_to_all(attended, 'heads', split_axis=1, concat_axis=0, tiled=True)]
    dot_general x9 -> x0, matrix products: 46.7 us -> none  [the longest x1 12.9 us: local(): jnp.dot(hidden, down_weight, preferred_element_type=jnp.float32)]
    reduce_scatter x1 -> x0, waiting for transfers between devices: 43.9 us -> none  [local(): lax.psum_scatter(jnp.dot(hidden, down_weight, preferred_element_type=jnp....]
    all_gather x2 -> x0, blocking collectives: 34 us -> none  [merged(): pieces = jax.tree.map(lambda part: lax.all_gather(part, axis), value)]
    all_to_all x5 -> x0, starting transfers between devices: 27.2 us -> none  [the longest x1 6.23 us: local(): lax.all_to_all(row_max.reshape(head_count, row_block, group_size), 'heads...]
  transfers between devices with their start and end apart: 8 -> 0, of which waited for: 7 -> 0; matrix products, arithmetic and copies ran while one was open for 3% -> 0% of each run, Pallas kernels for 0% -> 0%
where the time goes in v1:
time: 131 us
  Pallas kernels  130 us (99%)
  local copies, waits for them, and re-layouts  1.67 us (1%)
    pallas_call x1, Pallas kernels, fused(): pl.pallas_call(fused_kernel, out_shape=jax.ShapeDtypeStruct((2, block, de...  130 us

profile of v1, /device:TPU:17, one launch (start us, length us, event | category | flops | bytes accessed | tf_op | source)
XLA Modules:
  0.0 131.3 jit_solution(14871966592306229479)
XLA Ops:
  0.0 129.6 %shard_map.91 = bf16[2,32,2048]{2,1,0:T(8,128)(2,1)} custom-call(bf16[2,32,8192]{2,1,0:T(8,128)(2,1)} %bitcast.5, bf16[2,2,1024,128]{3,2,1,0:T(8,128)(2,1)} %kv_hbm.1, s32[2]{0:T(128)} %start_ref.1, bf16[2,32,2048]{2,1,0:T(8,128)(2,1)} %bitcast.6, bf16[2048,2048]{1,0:T(8,128)(2,1)} %wo_hbm.1, f32[1,2048]{1,0:T(1,128)} %bitcast.7, bf16[2048,3584]{1,0:T(8,128)(2,1)} %wg_hbm.1, ...), custom_call_target="tpu_custom_call" | custom-call | tf_op jit(solution)/shard_map/pallas_call | solution.py:554
  129.6 1.7 %copy.11 = bf16[64,2048]{1,0:T(8,128)(2,1)} copy(bf16[64,2048]{1,0:T(8,128)(2,1)} %bitcast.4) | data formatting | bytes 524288

commit v2 on v1

--- a/solution.py
+++ b/solution.py
@@ -282,13 +282,13 @@
     start = start_ref[c]
     positions = kvbuf.shape[1] * kvbuf.shape[2]
 
-    def head_body(k, half):
-        row = lax.broadcasted_iota(jnp.int32, (pair, 1), 0)
-        token = (row // block) * pair + half * block + row % block
-        col = lax.broadcasted_iota(jnp.int32, (pair, positions), 1)
+    def head_body(k):
+        row = lax.broadcasted_iota(jnp.int32, (span, 1), 0)
+        token = (row % pair // block) * pair + row // pair * block + row % block
+        col = lax.broadcasted_iota(jnp.int32, (span, positions), 1)
         allowed = col <= start + token
         s = lax.dot_general(
-            qbuf[half, :, lanes(k * HD, HD)], kvbuf[0].reshape(positions, HD),
+            qbuf[:, :, lanes(k * HD, HD)].reshape(span, HD), kvbuf[0].reshape(positions, HD),
             (((1,), (1,)), ((), ())), preferred_element_type=jnp.float32,
         ) * scale
         s = jnp.where(allowed, s, NEG_FILL)
@@ -298,8 +298,8 @@
             p.astype(jnp.bfloat16), kvbuf[1].reshape(positions, HD),
             preferred_element_type=jnp.float32,
         )
-        attn[half, subl(c * pair, pair), lanes(x * width + k * HD, HD)] = (o / total).astype(
-            jnp.bfloat16
+        attn[:, subl(c * pair, pair), lanes(x * width + k * HD, HD)] = (
+            (o / total).astype(jnp.bfloat16).reshape(2, pair, HD)
         )
 
     piece = width // 4
@@ -309,8 +309,7 @@
 
     def attn_body(ch, carry):
         for k in range(piece // HD):
-            for half in (0, 1):
-                head_body(ch * (piece // HD) + k, half)
+            head_body(ch * (piece // HD) + k)
         mine = attn_block(c, x, ch)
         remote(mine, mine, asx.at[ch], arx.at[ch], h, chip_peer).start()
         remote(mine, mine, asc.at[ch], arc.at[ch], h, core_peer).start()
@@ -342,11 +341,13 @@
     res_load.wait()
     cols = 512
 
-    def z_copy(half, d, target, ss, rs):
+    def z_copy(half, d, n, ss, rs):
         hh = ring(d)
+        at = lanes(n * cols, cols)
+        slot = 3 * n + d - 1
         return remote(
-            zsend.at[half, subl(hh * block, block), :], target.at[half, d - 1],
-            ss.at[half, d - 1], rs.at[half, d - 1], hh, r,
+            zsend.at[half, subl(hh * block, block), at], zrecv.at[half, d - 1, :, at],
+            ss.at[half, slot], rs.at[half, slot], hh, r,
         )
 
     def project_body(half, carry):
@@ -355,11 +356,11 @@
                 attn[half], wo[:, lanes(n * cols, cols)], preferred_element_type=jnp.float32
             )
             zsend[half, :, lanes(n * cols, cols)] = part.astype(jnp.bfloat16)
+            for d in (2, 1, 3):
+                z_copy(half, d, n, zss, zrs).start()
             return inner
 
         lax.fori_loop(0, depth // cols, chunk, 0)
-        for d in (2, 1, 3):
-            z_copy(half, d, zrecv, zss, zrs).start()
         return carry
 
     lax.fori_loop(0, 2, project_body, 0)
@@ -370,13 +371,17 @@
         return remote(mine, mine, rss.at[half, d - 1], rrs.at[half, d - 1], ring(d), r)
 
     def resid_body(half, carry):
-        for d in (1, 2, 3):
-            z_copy(half, d, zrecv, zss, zrs).wait_recv()
-        total = zsend[half, subl(h * block, block), :].astype(jnp.float32)
-        for d in (1, 2, 3):
-            total = total + zrecv[half, d - 1].astype(jnp.float32)
-        total = total + res[half].astype(jnp.float32)
-        resid[half, subl(h * block, block), :] = total.astype(jnp.bfloat16)
+        def chunk(n, inner):
+            at = lanes(n * cols, cols)
+            total = zsend[half, subl(h * block, block), at].astype(jnp.float32)
+            total = total + res[half, :, at].astype(jnp.float32)
+            for d in (1, 2, 3):
+                z_copy(half, d, n, zss, zrs).wait_recv()
+                total = total + zrecv[half, d - 1, :, at].astype(jnp.float32)
+            resid[half, subl(h * block, block), at] = total.astype(jnp.bfloat16)
+            return inner
+
+        lax.fori_loop(0, depth // cols, chunk, 0)
         for d in (2, 1, 3):
             r_copy(half, d, h).start()
         return carry
@@ -419,15 +424,13 @@
             for xx in (0, 1):
                 g_copy(0, xx).wait_send()
 
-        def partner(i, inner):
-            xx = lax.rem(1 - x + i, 2)
+        def partner(xx):
             g, u = both(2 * xx + 1 - c)
             gsend[xx, :, 0:quarter] = g.astype(jnp.bfloat16)
             gsend[xx, :, quarter:] = u.astype(jnp.bfloat16)
             g_copy(half, xx).start()
-            return inner
-
-        lax.fori_loop(0, 2, partner, 0)
+
+        partner(1 - x)
         g, u = both(2 * (1 - x) + c)
         g_copy(half, 1 - x).wait_recv()
         grecv[half, 1 - x, :, 0:quarter] = (
@@ -440,6 +443,7 @@
         sq_copy(half).wait_recv()
         sqr[half] = sqs[half] + sqr[half]
         sq_copy2(half).start()
+        partner(x)
         g, u = both(2 * x + c)
         g_copy(half, x).wait_recv()
         grecv[half, x, :, 0:quarter] = (
@@ -478,8 +482,13 @@
     def down_body(half, carry):
         h_copy(half, chip_peer, hsx, hrx, chip_peer).wait_recv()
         h_copy(half, chip_peer, hsf, hrf, core_peer).start()
-        for d in (1, 2, 3):
-            z_copy(half, d, zrecv, zss, zrs).wait_send()
+
+        def sent(n, inner):
+            for d in (1, 2, 3):
+                z_copy(half, d, n, zss, zrs).wait_send()
+            return inner
+
+        lax.fori_loop(0, depth // cols, sent, 0)
         h_copy(half, core_peer, hsc, hrc, core_peer).wait_recv()
         h_copy(half, 2 * (1 - x) + 1 - c, hsf, hrf, core_peer).wait_recv()
 
@@ -489,23 +498,27 @@
                 hid[half, :, 0:first], wo[:, at], preferred_element_type=jnp.float32
             ) + jnp.dot(hid[half, :, first:], wd2[:, at], preferred_element_type=jnp.float32)
             zsend[half, :, at] = part.astype(jnp.bfloat16)
+            for d in (2, 1, 3):
+                z_copy(half, d, n, dss, drs).start()
             return inner
 
         lax.fori_loop(0, depth // cols, chunk, 0)
-        for d in (2, 1, 3):
-            z_copy(half, d, zrecv, dss, drs).start()
         return carry
 
     lax.fori_loop(0, 2, down_body, 0)
 
     def final_body(half, carry):
-        for d in (1, 2, 3):
-            z_copy(half, d, zrecv, dss, drs).wait_recv()
-        total = zsend[half, subl(h * block, block), :].astype(jnp.float32)
-        for d in (1, 2, 3):
-            total = total + zrecv[half, d - 1].astype(jnp.float32)
-        total = total + resid[half, subl(h * block, block), :].astype(jnp.float32)
-        out_ref[half] = total.astype(jnp.bfloat16)
+        def chunk(n, inner):
+            at = lanes(n * cols, cols)
+            total = zsend[half, subl(h * block, block), at].astype(jnp.float32)
+            total = total + resid[half, subl(h * block, block), at].astype(jnp.float32)
+            for d in (1, 2, 3):
+                z_copy(half, d, n, dss, drs).wait_recv()
+                total = total + zrecv[half, d - 1, :, at].astype(jnp.float32)
+            out_ref[half, :, at] = total.astype(jnp.bfloat16)
+            return inner
+
+        lax.fori_loop(0, depth // cols, chunk, 0)
         return carry
 
     lax.fori_loop(0, 2, final_body, 0)
@@ -520,7 +533,8 @@
     def drain(half, carry):
         for d in (1, 2, 3):
             r_copy(half, d, h).wait_send()
-            z_copy(half, d, zrecv, dss, drs).wait_send()
+            for n in range(depth // cols):
+                z_copy(half, d, n, dss, drs).wait_send()
         sq_copy(half).wait_send()
         sq_copy2(half).wait_send()
         x_copy(half).wait_send()
@@ -581,10 +595,10 @@
             vmem((2, span, 128), f32),
             dma((8,)), dma((3,)), dma((2,)), dma((1,)), dma((1,)),
             dma((4,)), dma((4,)), dma((4,)), dma((4,)), dma((4,)), dma((4,)),
-            dma((2, 3)), dma((2, 3)), dma((2, 3)), dma((2, 3)),
+            dma((2, 12)), dma((2, 12)), dma((2, 3)), dma((2, 3)),
             dma((2, 2)), dma((2, 2)), dma((2,)), dma((2,)), dma((2, 2)), dma((2, 2)),
             dma((2,)), dma((2,)), dma((2,)), dma((2,)), dma((2,)), dma((2,)),
-            dma((2, 3)), dma((2, 3)),
+            dma((2, 12)), dma((2, 12)),
         ],
         compiler_params=pltpu.CompilerParams(
             collective_id=0, has_side_effects=True, vmem_limit_bytes=63 * 1024 * 1024

time: 131 us -> 126 us (0.962); the launches traced: 131 us -> 125 us
  Pallas kernels: 130 us -> 123 us
    pallas_call x1, Pallas kernels: 130 us -> 123 us  [fused(): pl.pallas_call(fused_kernel, out_shape=jax.ShapeDtypeStruct((2, block, de...]
where the time goes in v2:
time: 126 us; the launch traced here: 125 us
  Pallas kernels  123 us (98%)
  local copies, waits for them, and re-layouts  1.67 us (1%)
    pallas_call x1, Pallas kernels, fused(): pl.pallas_call(fused_kernel, out_shape=jax.ShapeDtypeStruct((2, block, de...  123 us

profile of v2, /device:TPU:17, one launch (start us, length us, event | category | flops | bytes accessed | tf_op | source)
XLA Modules:
  0.0 124.9 jit_solution(7249270977719690917)
XLA Ops:
  0.0 123.2 %shard_map.91 = bf16[2,32,2048]{2,1,0:T(8,128)(2,1)} custom-call(bf16[2,32,8192]{2,1,0:T(8,128)(2,1)} %bitcast.5, bf16[2,2,1024,128]{3,2,1,0:T(8,128)(2,1)} %kv_hbm.1, s32[2]{0:T(128)} %start_ref.1, bf16[2,32,2048]{2,1,0:T(8,128)(2,1)} %bitcast.6, bf16[2048,2048]{1,0:T(8,128)(2,1)} %wo_hbm.1, f32[1,2048]{1,0:T(1,128)} %bitcast.7, bf16[2048,3584]{1,0:T(8,128)(2,1)} %wg_hbm.1, ...), custom_call_target="tpu_custom_call" | custom-call | tf_op jit(solution)/shard_map/pallas_call | solution.py:568
  123.3 1.7 %copy.11 = bf16[64,2048]{1,0:T(8,128)(2,1)} copy(bf16[64,2048]{1,0:T(8,128)(2,1)} %bitcast.4) | data formatting | bytes 524288
